TPU v7x, 32 devices: a whole 2x2x4 slice. The times are simulated.
32 devices in a mesh: lon: 8 (over y, x, core), lat: 4 (over z).
Axes of the slice: x: 2, y: 2, z: 4, core: 2. Of those that a mesh axis runs over, the one named last changes fastest.
Arguments:
- temp: float32 [6, 1536, 2048], P(None, 'lat', 'lon'), may hold values from -6 to 6
- salt: float32 [6, 1536, 2048], P(None, 'lat', 'lon'), may hold values from 32 to 36
- east_vel: float32 [6, 1536, 2048], P(None, 'lat', 'lon'), may hold values from -0.2 to 0.2
- north_vel: float32 [6, 1536, 2048], P(None, 'lat', 'lon'), may hold values from -0.2 to 0.2
- land_mask: int32 [1536, 2048], P('lat', 'lon'), may hold values 0 or 1
- ice_mask: int32 [1536, 2048], P('lat', 'lon'), may hold values 0 or 1
- ice_u: float32 [1536, 2048], P('lat', 'lon'), may hold values from -3 to 3
- ice_v: float32 [1536, 2048], P('lat', 'lon'), may hold values from -3 to 3
- ice_pressure_field: float32 [1536, 2048], P('lat', 'lon'), may hold values from 1 to 3
- wind_x: float32 [1536, 2048], P('lat', 'lon'), may hold values from -3 to 3
- wind_y: float32 [1536, 2048], P('lat', 'lon'), may hold values from -3 to 3
Outputs:
- temp_out: float32 [6, 1536, 2048], P(None, 'lat', 'lon')
- salt_out: float32 [6, 1536, 2048], P(None, 'lat', 'lon')
- ice_u_out: float32 [1536, 2048], P('lat', 'lon')
- ice_v_out: float32 [1536, 2048], P('lat', 'lon')
All inputs are finite; a program needn't handle non-finite values. No bound on the sum of `land_mask` or of `ice_mask` on one device may be relied on, other than what follows from the above.
Results may differ from a plain program's by a relative error of at most 0.0003.
Values sent between devices are 32-bit elements; how exact they have to be, the bound alone decides.
No kernel may reach another device: no remote copies, remote signals or barrier semaphores. Data moves between devices by JAX's collectives and lax.ppermute only.
A program may use at most 192 MiB of HBM per device.

v0:
```python
import jax
import jax.numpy as jnp
from jax import lax
from jax.experimental import pallas as pl
from jax.experimental.pallas import tpu as pltpu
from jax.sharding import PartitionSpec as P

SUBCYCLES = 4
HEAT_RATE = 0.1
SALT_RATE = 0.5
FREEZE_SLOPE = 0.054
DIAGONAL = 1.5
HALO = 2 * SUBCYCLES
LANES = 128
SUBLANES = 8
ICE = 6
FOLD_SIGN = (-1.0, -1.0, 1.0, 1.0, -1.0, -1.0)
TRACER_LANE = 64
F32 = jnp.float32


def lane_ids():
    return lax.broadcasted_iota(jnp.int32, (SUBLANES, LANES), 1)


def sublane_ids():
    return lax.broadcasted_iota(jnp.int32, (SUBLANES, LANES), 0)


def turn(x, shift, axis=1):
    shift = shift % x.shape[axis]
    return pltpu.roll(x, shift, axis) if shift else x


def cut(t):
    return slice(LANES * t, LANES * (t + 1))


def ice_fields(land, ice, u, v, pressure, wind_x, wind_y, ocean_u, ocean_v):
    covered = land.astype(F32) * ice.astype(F32)
    return (u * covered, v * covered, pressure, covered, wind_x + ocean_u, wind_y + ocean_v)


def east_columns(fields, lane):
    packed = jnp.zeros((SUBLANES, LANES), F32)
    for f, tile in enumerate(fields):
        start = HALO * f + 2 * HALO
        moved = turn(tile, start - (LANES - HALO))
        packed = jnp.where((lane >= start) & (lane < start + HALO), moved, packed)
    return packed


def west_columns(fields, lane):
    packed = jnp.zeros((SUBLANES, LANES), F32)
    for f, tile in enumerate(fields):
        start = HALO * f
        packed = jnp.where((lane >= start) & (lane < start + HALO), turn(tile, start), packed)
    return packed


def sublane_rows(rows):
    return (rows + 2 * HALO) // SUBLANES | 1


class Trailing:
    def __init__(self, window):
        self.window, self.waiting = window, []

    def add(self, writes):
        self.waiting.append(writes)
        while len(self.waiting) > self.window:
            self.flush(self.waiting.pop(0))

    def finish(self):
        for writes in self.waiting:
            self.flush(writes)

    @staticmethod
    def flush(writes):
        for ref, where, value in writes:
            ref[where] = value


def straight(steps, body, window, size):
    size = max(c for c in range(1, size + 1) if steps % c == 0)

    def run(n, carry):
        pending = Trailing(window)
        for j in range(size):
            pending.add(body(n * size + j))
        pending.finish()
        return carry

    if size == steps:
        run(0, 0)
    else:
        lax.fori_loop(0, steps // size, run, 0)


def in_groups_of(group, steps, body, size=0):
    size = max(c for c in range(1, (size or group) + 1) if steps % c == 0)

    def run(n, carry):
        for start in range(0, size, group):
            writes = []
            for j in range(start, min(start + group, size)):
                writes += body(n * size + j)
            Trailing.flush(writes)
        return carry

    lax.fori_loop(0, steps // size, run, 0)


def tile_rows(k, offset=0):
    start = k * SUBLANES
    if not isinstance(k, int):
        start = pl.multiple_of(start, SUBLANES)
    return pl.ds(start + offset if offset else start, SUBLANES)


def rows_kernel(levels, *refs):
    tops, bottoms = refs[0:12], refs[12:24]
    second_ref, first_ref = refs[24:26]
    even = lax.rem(lax.axis_index("lat"), 2) == 0

    def message(group, row, northward):
        land, ice, u, v, pressure, wind_x, wind_y, east, north, temp, salt = (
            r for r in group[:11]
        )
        fields = ice_fields(
            land[...], ice[...], u[...], v[...], pressure[...], wind_x[...], wind_y[...],
            east[0], north[0],
        )
        sea = land[row : row + 1, :].astype(F32)
        parts = list(fields) + [temp[:, row, :], salt[:, row, :]]
        if northward:
            parts.append(north[:, row, :] * sea)
        else:
            parts.append(jnp.broadcast_to(sea, (levels, sea.shape[1])))
        return parts

    top = message(tops, SUBLANES - 1, True)
    bottom = message(bottoms, 0, False)
    at = 0
    for t, b in zip(top, bottom):
        size = t.shape[0]
        first_ref[at : at + size, :] = jnp.where(even, t, b)
        second_ref[at : at + size, :] = jnp.where(even, b, t)
        at += size
    pad = first_ref.shape[0] - at
    if pad:
        first_ref[at:, :] = jnp.zeros((pad, first_ref.shape[1]), F32)
        second_ref[at:, :] = jnp.zeros((pad, second_ref.shape[1]), F32)


def pack_rows(arrays, levels, rows, cols, height):
    temp, salt, east, north, land, ice, u, v, pressure, wind_x, wind_y = arrays
    operands = [land, ice, u, v, pressure, wind_x, wind_y, east, north, temp, salt, land]
    last = rows // SUBLANES - 1

    def spec(array, block, count):
        if array.ndim == 2:
            return pl.BlockSpec((SUBLANES, cols), lambda _: (block, 0))
        return pl.BlockSpec((count, SUBLANES, cols), lambda _: (0, block, 0))

    counts = [1] * 7 + [1, levels, levels, levels, 1]
    specs = [spec(a, last, c) for a, c in zip(operands, counts)]
    specs += [spec(a, 0, c) for a, c in zip(operands, counts)]
    out = jax.ShapeDtypeStruct((height, cols), F32)
    return pl.pallas_call(
        lambda *refs: rows_kernel(levels, *refs),
        grid=(1,),
        in_specs=specs,
        out_specs=[pl.BlockSpec((height, cols), lambda _: (0, 0))] * 2,
        out_shape=[out, out],
        name="edge_rows",
        compiler_params=pltpu.CompilerParams(vmem_limit_bytes=8 << 20),
        cost_estimate=pl.CostEstimate(flops=100000, bytes_accessed=1 << 20, transcendentals=0),
    )(*[in_hbm(a) for a in operands + operands])


def on_even_lon():
    return lax.rem(lax.axis_index("lon"), 2) == 0


def columns_kernel(levels, land, ice, u, v, pressure, wind_x, wind_y, east, north, temp, salt,
                   tracer_out, speed_out, sea_out, field_out, inter_out, intra_out, sem):
    lane = lane_ids()
    even = on_even_lon()
    rows = sea_out.shape[1]
    tiles = sea_out.shape[0]
    tracers = 2 * levels
    first_lane = TRACER_LANE
    mask_lane = TRACER_LANE + 2 * tracers

    copies = []
    for n, ref in enumerate((temp, salt, east, north)):
        out = tracer_out if n < 2 else speed_out
        for t in range(tiles):
            copies.append(
                pltpu.make_async_copy(
                    ref.at[..., pl.ds(LANES * t, LANES)],
                    out.at[pl.ds(levels * (n % 2), levels), t],
                    sem.at[n, t],
                )
            )
    for copy in copies:
        copy.start()

    whole = slice(None)

    def messages(put, eastward, westward):
        return [
            (inter_out, (put, whole), jnp.where(even, westward, eastward)),
            (intra_out, (put, whole), jnp.where(even, eastward, westward)),
        ]

    def packed(put):
        inter, intra = inter_out[put, :], intra_out[put, :]
        return jnp.where(even, intra, inter), jnp.where(even, inter, intra)

    def ice_part(k):
        at, put = tile_rows(k), tile_rows(k + 1)
        writes, fields = [], []
        for t in range(tiles):
            c = cut(t)
            fields.append(
                ice_fields(
                    *[r[at, c] for r in (land, ice, u, v, pressure, wind_x, wind_y)],
                    east[0, at, c], north[0, at, c],
                )
            )
            writes.append((sea_out, (t, at, whole), land[at, c].astype(F32)))
            for f in range(ICE):
                writes.append((field_out, (f, t, put, whole), fields[t][f]))
        return writes + messages(
            put, east_columns(fields[-1], lane), west_columns(fields[0], lane)
        )

    in_groups_of(4, rows // SUBLANES, ice_part)

    def tracer_part(k):
        at, put = tile_rows(k), tile_rows(k + 1)
        eastward, westward = packed(put)
        for f in range(tracers):
            ref, l, to = (temp, salt)[f // levels], f % levels, first_lane + 2 * f
            eastward = jnp.where(
                lane == to, turn(ref[l, at, cut(tiles - 1)], to - (LANES - 1)), eastward
            )
            westward = jnp.where(lane == to, turn(ref[l, at, cut(0)], to), westward)
        return messages(put, eastward, westward)

    in_groups_of(12, rows // SUBLANES, tracer_part)

    def speed_part(k):
        at, put = tile_rows(k), tile_rows(k + 1)
        masked = (lane >= mask_lane) & (lane < mask_lane + 2 * tracers)
        speeds = jnp.zeros((SUBLANES, LANES), F32)
        for f in range(levels):
            to = mask_lane + 2 * f
            speeds = jnp.where(
                lane == to, turn(east[f, at, cut(tiles - 1)], to - (LANES - 1)), speeds
            )
        speeds = speeds + turn(speeds, 2 * levels)
        last = land[at, LANES * tiles - 1 : LANES * tiles].astype(F32)
        first = jnp.broadcast_to(land[at, 0:1].astype(F32), (SUBLANES, LANES))
        eastward, westward = packed(put)
        eastward = jnp.where(masked, speeds * last, eastward)
        westward = jnp.where(masked, first, westward)
        return messages(put, eastward, westward)

    in_groups_of(12, rows // SUBLANES, speed_part)
    end = HALO + rows
    blank = jnp.zeros((field_out.shape[2] - end, LANES), F32)
    for t in range(tiles):
        for f in range(ICE):
            field_out[f, t, end:, :] = blank
    for ref in (inter_out, intra_out):
        ref[end:, :] = blank
    for copy in copies:
        copy.wait()


def in_vmem(x):
    return pltpu.with_memory_space_constraint(x, pltpu.VMEM)


def in_hbm(x):
    return pltpu.with_memory_space_constraint(x, pltpu.HBM)


def resident(*shape):
    return pltpu.VMEM(shape, F32)


VMEM_SPEC = pl.BlockSpec(memory_space=pltpu.VMEM)
ANY_SPEC = pl.BlockSpec(memory_space=pl.ANY)


def load_and_pack_columns(arrays, levels, rows, cols):
    temp, salt, east, north, land, ice, u, v, pressure, wind_x, wind_y = arrays
    tiles = cols // LANES
    message = resident(sublane_rows(rows) * SUBLANES, LANES)
    deep = resident(2 * levels, tiles, rows, LANES)
    return pl.pallas_call(
        lambda *refs: columns_kernel(levels, *refs),
        in_specs=[VMEM_SPEC] * 11,
        out_specs=[VMEM_SPEC] * 6,
        out_shape=[
            deep, deep, resident(tiles, rows, LANES),
            resident(ICE, tiles, sublane_rows(rows) * SUBLANES, LANES), message, message,
        ],
        scratch_shapes=[pltpu.SemaphoreType.DMA((4, tiles))],
        name="edge_columns",
        compiler_params=pltpu.CompilerParams(vmem_limit_bytes=4 << 20),
        cost_estimate=pl.CostEstimate(flops=5000000, bytes_accessed=12 << 20, transcendentals=0),
    )(*[in_vmem(a) for a in (land, ice, u, v, pressure, wind_x, wind_y, east, north, temp, salt)])


def halo_kernel(levels, rows, second, first, field_in, inter_in, intra_in,
                halo_ref, field_out, inter_out, intra_out):
    lat = lax.axis_index("lat")
    even = lax.rem(lat, 2) == 0
    top = lat == lax.axis_size("lat") - 1
    lane, sublane = lane_ids(), sublane_ids()
    tiles = field_out.shape[1]
    south_fields, north_fields = [], []
    for f in range(ICE):
        at = slice(HALO * f, HALO * (f + 1))
        north_row, south_row = [], []
        for t in range(tiles):
            cols = slice(LANES * t, LANES * (t + 1))
            mirror = slice(LANES * (tiles - 1 - t), LANES * (tiles - t))
            south = jnp.where(even, second[at, cols], first[at, cols])
            plain = jnp.where(even, first[at, cols], second[at, cols])
            turned = jnp.take_along_axis(second[at, mirror], LANES - 1 - lane, axis=1)
            turned = jnp.take_along_axis(turned, SUBLANES - 1 - sublane, axis=0)
            north = jnp.where(top, turned * FOLD_SIGN[f], plain)
            field_out[f, t, 0:HALO, :] = south
            field_out[f, t, rows + HALO : rows + 2 * HALO, :] = north
            south_row.append(south)
            north_row.append(north)
        south_fields.append(south_row)
        north_fields.append(north_row)
    rest = slice(HALO * ICE, first.shape[0])
    for t in range(tiles):
        c = cut(t)
        halo_ref[0, t] = jnp.where(even, second[rest, c], first[rest, c])
        halo_ref[1, t] = jnp.where(top, 0.0, jnp.where(even, first[rest, c], second[rest, c]))
    for at, fields in ((0, south_fields), (rows + HALO, north_fields)):
        eastward = east_columns([f[-1] for f in fields], lane)
        westward = west_columns([f[0] for f in fields], lane)
        inter_out[at : at + HALO, :] = jnp.where(on_even_lon(), westward, eastward)
        intra_out[at : at + HALO, :] = jnp.where(on_even_lon(), eastward, westward)


def merge_halo(second, first, fields, inter_msg, intra_msg, levels, rows):
    height, cols = first.shape
    return pl.pallas_call(
        lambda *refs: halo_kernel(levels, rows, *refs),
        in_specs=[VMEM_SPEC] * 5,
        out_specs=[VMEM_SPEC] * 4,
        out_shape=[
            resident(2, cols // LANES, height - HALO * ICE, LANES), resident(*fields.shape),
            resident(*inter_msg.shape), resident(*intra_msg.shape),
        ],
        input_output_aliases={2: 1, 3: 2, 4: 3},
        name="halo_rows",
        compiler_params=pltpu.CompilerParams(vmem_limit_bytes=8 << 20),
        cost_estimate=pl.CostEstimate(flops=100000, bytes_accessed=1 << 19, transcendentals=0),
    )(second, first, in_vmem(fields), in_vmem(inter_msg), in_vmem(intra_msg))


def advect_kernel(levels, row_total, tracer_ref, speed_ref, sea, halo, field_ref,
                  out, base_u, base_v, third, force, push_x, push_y, turn_a, turn_b,
                  mask_e, mask_n):
    tiles, rows = sea.shape[:2]
    count = rows // SUBLANES
    group = next(c for c in (12, 8, 4, 2) if count % c == 0)
    lane, sublane = lane_ids(), sublane_ids()
    extra_row = 2 * levels
    whole = slice(None)

    def rows_at(k, offset=0):
        start = pl.multiple_of(k * SUBLANES, SUBLANES)
        return pl.ds(start + offset if offset else start, SUBLANES)

    def row(side, index, t):
        return jnp.broadcast_to(halo[side, t, index : index + 1, :], (SUBLANES, LANES))

    def from_next(values):
        turned = [turn(v, -1) for v in values]
        return [
            jnp.where(lane == LANES - 1, turned[t + 1], turned[t]) if t + 1 < tiles else turned[t]
            for t in range(tiles)
        ]

    def from_last(values):
        turned = [turn(v, 1) for v in values]
        return [jnp.where(lane == 0, turned[t - 1], turned[t]) for t in range(tiles)]

    def in_groups(body, carry):
        def some(start, carry, last):
            writes = []
            for j in range(group):
                more, carry = body(start + j, last and j == group - 1, carry)
                writes += more
            for ref, where, value in writes:
                ref[where] = value
            return carry

        groups = count // group
        carry = lax.fori_loop(0, groups - 1, lambda n, c: some(n * group, c, False), carry)
        return some((groups - 1) * group, carry, True)

    def row_above(load, k, last, past):
        if not last:
            return load(rows_at(k, 1))
        return jnp.where(sublane == SUBLANES - 1, past, turn(load(rows_at(k)), -1, 0))

    def masks(k, last, carry):
        here = [sea[t, rows_at(k), :] for t in range(tiles)]
        beside = from_next(here)
        writes = []
        for t in range(tiles):
            above = row_above(lambda at, t=t: sea[t, at, :], k, last, row(1, extra_row, t))
            face = here[t] * beside[t]
            if t == tiles - 1:
                face = jnp.where(lane == LANES - 1, 0.0, face)
            writes.append((mask_e, (t, rows_at(k), whole), face))
            writes.append((mask_n, (t, rows_at(k), whole), here[t] * above))
        return writes, carry

    in_groups(masks, 0)
    for level in range(levels):
        entering = []
        for f in (level, levels + level):
            for t in range(tiles):
                speed = row(0, extra_row + level, t) * sea[t, 0:SUBLANES, :]
                start = tracer_ref[f, t, 0:SUBLANES, :]
                entering.append(speed * jnp.where(speed > 0, row(0, f, t), start))

        def body(k, last, carry, level=level):
            at = rows_at(k)
            fast_e = [speed_ref[level, t, at, :] * mask_e[t, at, :] for t in range(tiles)]
            fast_n = [speed_ref[levels + level, t, at, :] * mask_n[t, at, :] for t in range(tiles)]
            writes, result = [], []
            for f in (level, levels + level):
                here = [tracer_ref[f, t, at, :] for t in range(tiles)]
                beside = from_next(here)
                flux_e = [
                    fast_e[t] * jnp.where(fast_e[t] > 0, here[t], beside[t]) for t in range(tiles)
                ]
                before = from_last(flux_e)
                for t in range(tiles):
                    above = row_above(
                        lambda at, f=f, t=t: tracer_ref[f, t, at, :], k, last, row(1, f, t)
                    )
                    flux_n = fast_n[t] * jnp.where(fast_n[t] > 0, here[t], above)
                    turned = turn(flux_n, 1, 0)
                    below = jnp.where(sublane == 0, carry[len(result)], turned)
                    value = here[t] - ((flux_e[t] - before[t]) + (flux_n - below))
                    writes.append((out, (f, t, at, whole), value))
                    result.append(turned)
            return writes, tuple(result)

        in_groups(body, tuple(entering))
    spread_fields(rows, row_total, field_ref, base_u, base_v, third, force, push_x, push_y,
                  turn_a, turn_b)


def spread(ref, i, count, *lead):
    return ref[(*lead, pl.ds(i, SUBLANES, stride=count), slice(None))]


def wrap(ref, count, lanes=slice(None)):
    ref[0, :, lanes] = turn(ref[count, :, lanes], 1, 0)
    ref[count + 1, :, lanes] = turn(ref[1, :, lanes], -1, 0)


def spread_fields(rows, row_total, field_ref, base_u, base_v, third, force, push_x, push_y,
                  turn_a, turn_b):
    tiles = field_ref.shape[1]
    count = sublane_rows(rows)
    lane, sublane = lane_ids(), sublane_ids()
    lat = lax.axis_index("lat")

    def body(i):
        per_tile = [[spread(field_ref, i, count, f, t) for f in range(ICE)] for t in range(tiles)]
        extra = []
        for f in range(ICE):
            low, high = per_tile[0][f], per_tile[-1][f]
            middle = turn(jnp.where(lane < LANES // 2, high, low), 48)
            x = jnp.where(lane < 32, low, middle)
            extra.append(jnp.where(lane >= 64, turn(high, -24), x))
        writes = []
        for t, fields in enumerate(per_tile + [extra]):
            u0, v0, strength, covered, drive_x, drive_y = fields
            writes.append((base_u, (i + 1, slice(None), cut(t)), u0))
            writes.append((base_v, (i + 1, slice(None), cut(t)), v0))
            writes.append((third, (i, slice(None), cut(t)), covered * (1.0 / 3.0)))
            writes.append((force, (i, slice(None), cut(t)), strength * covered * (1.0 / 12.0)))
            writes.append((push_x, (i, slice(None), cut(t)), 0.5 * drive_x))
            writes.append((push_y, (i, slice(None), cut(t)), 0.5 * drive_y))
        y = lat * rows - HALO + sublane * count + i
        y = jnp.where(y >= row_total, 2 * row_total - 1 - y, y)
        coriolis = 0.5 * (2 * y + 1 - row_total).astype(F32) / row_total
        turning = 0.5 * coriolis
        scale = 3.0 / (DIAGONAL * DIAGONAL + turning * turning)
        writes.append((turn_a, (i,), DIAGONAL * scale))
        writes.append((turn_b, (i,), turning * scale))
        return writes

    in_groups_of(3, count, body, 17)
    wrap(base_u, count)
    wrap(base_v, count)


def advect(tracers, speeds, sea, halo, fields, levels, row_total):
    tiles, rows = sea.shape[:2]
    count = sublane_rows(rows)
    wide = LANES * (tiles + 1)
    looped = resident(count + 2, SUBLANES, wide)
    plain = resident(count, SUBLANES, wide)
    narrow = resident(count, SUBLANES, LANES)
    return pl.pallas_call(
        lambda *refs: advect_kernel(levels, row_total, *refs),
        in_specs=[VMEM_SPEC] * 5,
        out_specs=[VMEM_SPEC] * 9,
        out_shape=[
            resident(*tracers.shape), looped, looped, plain, plain, plain, plain, narrow, narrow,
        ],
        scratch_shapes=[pltpu.VMEM((tiles, rows, LANES), F32)] * 2,
        name="advect",
        compiler_params=pltpu.CompilerParams(vmem_limit_bytes=8 << 20),
        cost_estimate=pl.CostEstimate(flops=30000000, bytes_accessed=16 << 20, transcendentals=0),
    )(*[in_vmem(a) for a in (tracers, speeds, sea, halo, fields)])


def ice_kernel(levels, rows, *refs):
    (covered_in, tracers_in, speeds_in, inter_own, intra_own, inter_in, intra_in,
     base_u, base_v, third, force, push_x, push_y, turn_a, turn_b,
     temp_out, salt_out, u_out, v_out,
     moved, done, vel_u, vel_v, str_a, str_b, str_c,
     third_x, force_x, push_x_x, push_y_x, edges,
     out_sem, vel_sem) = refs
    tiles = tracers_in.shape[1]
    count = sublane_rows(rows)
    tracers = 2 * levels
    lane = lane_ids()
    own = pl.ds(HALO, rows)
    wide = tiles + 1
    whole = slice(None)

    even = on_even_lon()

    def sides(inter, intra):
        return jnp.where(even, inter, intra), jnp.where(even, intra, inter)

    def edge_fluxes(k):
        at, put = tile_rows(k + 1), tile_rows(k)
        west, east_side = sides(inter_in[at, :], intra_in[at, :])
        mine_w, mine_e = sides(inter_own[at, :], intra_own[at, :])
        speed = turn(west, -2 * tracers)
        inflow = speed * jnp.where(speed > 0, west, mine_w) * turn(mine_w, -2 * tracers)
        speed = turn(mine_e, -2 * tracers)
        outflow = speed * jnp.where(speed > 0, mine_e, east_side) * turn(east_side, -2 * tracers)
        flux = jnp.where(lane % 2 == TRACER_LANE % 2, inflow, turn(outflow, -1))
        return [(edges, (put, whole), flux)]

    straight(rows // SUBLANES, edge_fluxes, 8, 24)

    def fixed(f, put):
        flux = turn(edges[put, :], -(TRACER_LANE + 2 * f))
        low = tracers_in[f, 0, put, :] + jnp.where(lane == 0, flux, 0.0)
        return low, tracers_in[f, tiles - 1, put, :] - jnp.where(lane == LANES - 1, flux, 0.0)

    def insert(i):
        west, east_side = sides(spread(inter_in, i, count), spread(intra_in, i, count))
        writes = []
        targets = (
            (base_u, vel_u, 1, tiles, 1.0), (base_v, vel_v, 1, tiles, 1.0),
            (force, force_x, 0, 0, 1.0), (third, third_x, 0, 0, 1.0 / 3.0),
            (push_x, push_x_x, 0, 0, 0.5), (push_y, push_y_x, 0, 0, 0.5),
        )
        beyond = []
        for f in range(ICE):
            start = HALO * f + 2 * HALO
            x = jnp.where((lane >= start) & (lane < start + HALO), west, east_side)
            beyond.append(turn(x, 104 - HALO * f))
        beyond[2] = beyond[2] * beyond[3] * (1.0 / 12.0)
        for x, (source, target, shift, t, factor) in zip(beyond, targets):
            x = x if factor == 1.0 else x * factor
            x = jnp.where(lane >= 104, x, source[i + shift, :, cut(tiles)])
            writes.append((target, (i + shift, whole, cut(t)), x))
        own_lanes = slice(0, LANES * tiles)
        for source, target in ((base_u, vel_u), (base_v, vel_v)):
            writes.append((target, (i + 1, whole, own_lanes), source[i + 1, :, own_lanes]))
        for ref in (str_a, str_b, str_c):
            writes.append((ref, (i + 1,), jnp.zeros(ref.shape[1:], F32)))
        return writes

    straight(count, insert, 3, 17)
    wrap(vel_u, count)
    wrap(vel_v, count)

    def constant(ref, extra, i, t):
        return ref[i, :, cut(t)] if t < tiles else extra[i]

    def load_once(ref, name, seen, j, t):
        if (name, j, t) not in seen:
            seen[name, j, t] = ref[(j, whole) if t is None else (j, whole, cut(t))]
        return seen[name, j, t]

    share = rows // SUBLANES // SUBCYCLES
    items = [(k, f) for k in range(share) for f in range(tracers)]

    def fix(step, i):
        for k, f in items[len(items) * i // count : len(items) * (i + 1) // count]:
            put = pl.ds(pl.multiple_of((step * share + k) * SUBLANES, SUBLANES), SUBLANES)
            low, high = fixed(f, put)
            moved[f, 0, put, :] = low
            moved[f, tiles - 1, put, :] = high

    def fixed_rows(step):
        part = pl.ds(pl.multiple_of(step * share * SUBLANES, SUBLANES), share * SUBLANES)
        return [
            pltpu.make_async_copy(
                moved.at[pl.ds(levels * n + 1, levels - 1), t, part, :],
                out.at[pl.ds(1, levels - 1), part, pl.ds(LANES * t, LANES)],
                out_sem.at[step, n, t],
            )
            for n, out in enumerate((temp_out, salt_out))
            for t in range(tiles)
        ]

    def strain_stress(step):
        seen = {}
        for i in range(count):
            for t in range(wide):
                u, v = (load_once(r, n, seen, i + 1, t) for n, r in enumerate((vel_u, vel_v)))
                dudx, dvdx = turn(u, -1) - turn(u, 1), turn(v, -1) - turn(v, 1)
                dudy, dvdy = (
                    load_once(r, n, seen, i + 2, t) - load_once(r, n, seen, i, t)
                    for n, r in enumerate((vel_u, vel_v))
                )
                div, ten, shr = dudx + dvdy, dudx - dvdy, dudy + dvdx
                square = div * div + 0.25 * (ten * ten + shr * shr) + 1.0
                base = constant(force, force_x, i, t)
                zeta = base * lax.rsqrt(square)
                quarter = 0.25 * zeta
                even = zeta * div - base
                odd = quarter * ten
                keep = constant(third, third_x, i, t)
                for ref, new in (
                    (str_a, even + odd), (str_b, even - odd), (str_c, quarter * shr)
                ):
                    ref[i + 1, :, cut(t)] = new + keep * ref[i + 1, :, cut(t)]
            fix(step, i)
        wrap(str_b, count)
        wrap(str_c, count)

    def momentum():
        seen = {}
        for i in range(count):
            ar, br = turn_a[i], turn_b[i]
            for t in range(wide):
                a = str_a[i + 1, :, cut(t)]
                s = load_once(str_c, 2, seen, i + 1, t)
                fx = (turn(a, -1) - turn(a, 1)) + (
                    load_once(str_c, 2, seen, i + 2, t) - load_once(str_c, 2, seen, i, t)
                )
                fy = (turn(s, -1) - turn(s, 1)) + (
                    load_once(str_b, 1, seen, i + 2, t) - load_once(str_b, 1, seen, i, t)
                )
                ru = (vel_u[i + 1, :, cut(t)] + constant(push_x, push_x_x, i, t)) + fx
                rv = (vel_v[i + 1, :, cut(t)] + constant(push_y, push_y_x, i, t)) + fy
                keep = constant(third, third_x, i, t)
                vel_u[i + 1, :, cut(t)] = (ar * ru + br * rv) * keep
                vel_v[i + 1, :, cut(t)] = (ar * rv - br * ru) * keep
        wrap(vel_u, count)
        wrap(vel_v, count)

    def subcycle(step, carry):
        strain_stress(step)
        for copy in fixed_rows(step):
            copy.start()
        momentum()
        return carry

    lax.fori_loop(0, SUBCYCLES, subcycle, 0)

    def gather(i):
        writes = []
        for n, ref in enumerate((vel_u, vel_v)):
            borders = ref[i + 1, :, cut(tiles)]
            middle, outer = turn(borders, -48), turn(borders, 24)
            low, high = ref[i + 1, :, cut(0)], ref[i + 1, :, cut(tiles - 1)]
            low = jnp.where(lane < HALO, borders, jnp.where(lane >= LANES - HALO, middle, low))
            high = jnp.where(lane < HALO, middle, jnp.where(lane >= LANES - HALO, outer, high))
            put = pl.ds(i, SUBLANES, stride=count)
            writes.append((done, (n, 0, put, whole), low))
            writes.append((done, (n, tiles - 1, put, whole), high))
        return writes

    straight(count, gather, 6, 51)
    finals = []
    for n, out in enumerate((u_out, v_out)):
        for t in range(tiles):
            finals.append(
                pltpu.make_async_copy(
                    done.at[n, t, own, :], out.at[:, pl.ds(LANES * t, LANES)], vel_sem.at[n, t]
                )
            )
            finals[-1].start()

    def warm(k):
        put, at = tile_rows(k), tile_rows(k + 1)
        writes = []
        for t in range(tiles):
            sst, sss = moved[0, t, put, :], moved[levels, t, put, :]
            slip_u = done[0, t, at, :] - speeds_in[0, t, put, :]
            slip_v = done[1, t, at, :] - speeds_in[levels, t, put, :]
            heat = HEAT_RATE * covered_in[3, t, at, :] * (1.0 + (slip_u * slip_u + slip_v * slip_v))
            heat = heat * (sst + FREEZE_SLOPE * sss)
            writes.append((moved, (0, t, put, whole), sst - heat))
            writes.append((moved, (levels, t, put, whole), sss - SALT_RATE * heat))
        return writes

    straight(rows // SUBLANES, warm, 6, 24)
    for n, out in enumerate((temp_out, salt_out)):
        for t in range(tiles):
            finals.append(
                pltpu.make_async_copy(
                    moved.at[levels * n, t],
                    out.at[0, :, pl.ds(LANES * t, LANES)],
                    out_sem.at[SUBCYCLES, n, t],
                )
            )
            finals[-1].start()
    for step in range(SUBCYCLES):
        finals += fixed_rows(step)
    for copy in finals:
        copy.wait()


def ice_and_edges(operands, levels, rows, cols):
    tiles = cols // LANES
    count = sublane_rows(rows)
    deep = jax.ShapeDtypeStruct((levels, rows, cols), F32)
    flat = jax.ShapeDtypeStruct((rows, cols), F32)
    looped = pltpu.VMEM((count + 2, SUBLANES, LANES * (tiles + 1)), F32)
    narrow = pltpu.VMEM((count, SUBLANES, LANES), F32)
    return pl.pallas_call(
        lambda *refs: ice_kernel(levels, rows, *refs),
        in_specs=[VMEM_SPEC] * len(operands),
        out_specs=[ANY_SPEC] * 4,
        out_shape=[deep, deep, flat, flat],
        scratch_shapes=[
            pltpu.VMEM((2 * levels, tiles, rows, LANES), F32),
            pltpu.VMEM((2, tiles, count * SUBLANES, LANES), F32),
            looped, looped, looped, looped, looped,
            narrow, narrow, narrow, narrow, pltpu.VMEM((rows, LANES), F32),
            pltpu.SemaphoreType.DMA((SUBCYCLES + 1, 2, tiles)),
            pltpu.SemaphoreType.DMA((2, tiles)),
        ],
        name="ice",
        compiler_params=pltpu.CompilerParams(vmem_limit_bytes=20 << 20),
        cost_estimate=pl.CostEstimate(flops=60000000, bytes_accessed=16 << 20, transcendentals=0),
    )(*[in_vmem(a) for a in operands])


def per_device(*arrays):
    levels, rows, cols = arrays[0].shape
    lon_count, lat_count = lax.axis_size("lon"), lax.axis_size("lat")
    assert cols == 2 * LANES and rows % (SUBLANES * SUBCYCLES) == 0
    assert lat_count % 2 == 0 and lon_count % 2 == 0
    height = -(-(HALO * ICE + 3 * levels) // SUBLANES) * SUBLANES

    def place(lat, lon):
        return lon * lat_count + lat

    first_pairs, second_pairs = [], []
    for lon in range(lon_count):
        for lat in range(lat_count):
            first_pairs.append((place(lat, lon), place(lat ^ 1, lon)))
            if lat == lat_count - 1:
                second_pairs.append((place(lat, lon), place(lat, lon_count - 1 - lon)))
            elif lat:
                second_pairs.append((place(lat, lon), place(((lat + 1) ^ 1) - 1, lon)))
    inter_pairs = [(i, (i - 1 if i % 2 == 0 else i + 1) % lon_count) for i in range(lon_count)]
    intra_pairs = [(i, i ^ 1) for i in range(lon_count)]
    second, first = pack_rows(arrays, levels, rows, cols, height)
    second = lax.ppermute(second, ("lon", "lat"), second_pairs)
    first = lax.ppermute(first, ("lon", "lat"), first_pairs)
    tracers, speeds, sea, fields, inter, intra = load_and_pack_columns(arrays, levels, rows, cols)
    halo, fields, inter, intra = merge_halo(second, first, fields, inter, intra, levels, rows)
    intra_in = lax.ppermute(intra, "lon", intra_pairs)
    inter_in = lax.ppermute(inter, "lon", inter_pairs)
    moved, *state = advect(tracers, speeds, sea, halo, fields, levels, rows * lat_count)
    return ice_and_edges(
        [fields, moved, speeds, inter, intra, inter_in, intra_in, *state], levels, rows, cols
    )


def solution(mesh):
    deep, flat = P(None, "lat", "lon"), P("lat", "lon")
    return jax.shard_map(
        per_device,
        mesh=mesh,
        in_specs=(deep,) * 4 + (flat,) * 7,
        out_specs=(deep, deep, flat, flat),
        check_vma=False,
    )
```

profile of v0, /device:TPU:0, one launch (start us, length us, event | category | flops | bytes accessed | tf_op | source)
XLA Modules:
  0.0 31.5 jit_solution(15763199032474562191)
XLA Ops:
  0.6 0.0 copy-start.10
  0.6 0.0 copy-start.9
  0.7 0.0 copy-start.8
  0.7 0.0 copy-start.7
  0.7 0.0 copy-start.6
  0.7 0.0 copy-start.5
  0.7 0.0 copy-start.4
  0.7 0.0 copy-start.1
  0.7 0.0 copy-start
  0.7 0.0 copy-start.3
  0.7 0.0 copy-start.2
  0.7 1.2 %edge_rows.1 = (f32[72,256]{1,0:T(8,128)S(1)}, f32[72,256]{1,0:T(8,128)S(1)}) custom-call(s32[384,256]{1,0:T(8,128)} %refs_0_.3, s32[384,256]{1,0:T(8,128)} %refs_1_.3, f32[384,256]{1,0:T(8,128)} %refs_2_.3, f32[384,256]{1,0:T(8,128)} %refs_3_.3, f32[384,256]{1,0:T(8,128)} %refs_4_.3, f32[384,256]{1,0:T(8,128)} %refs_5_.3, f32[384,256]{1,0:T(8,128)} %refs_6_.3, ...), custom_call_target="tpu_custom_call" | custom-call | flops 100000 | bytes 1048576 | tf_op jit(solution)/shard_map/edge_rows/pallas_call | solution.py:170
  1.9 0.8 %collective-permute-start = (f32[72,256]{1,0:T(8,128)S(1)}, f32[72,256]{1,0:T(8,128)S(1)}, u32[]{:S(2)}, u32[]{:S(2)}) collective-permute-start(f32[72,256]{1,0:T(8,128)S(1)} %get-tuple-element.25), channel_id=1, source_target_pairs={{1,2},{2,1},{3,31},{5,6},{6,5},{7,27},{9,10},{10,9},{11,23},{13,14... | collective-permute-start | bytes 221192 | tf_op jit(solution)/shard_map/ppermute | solution.py:794
  2.8 6.0 %collective-permute-start.1 = (f32[72,256]{1,0:T(8,128)S(1)}, f32[72,256]{1,0:T(8,128)S(1)}, u32[]{:S(2)}, u32[]{:S(2)}) collective-permute-start(f32[72,256]{1,0:T(8,128)S(1)} %get-tuple-element.26), channel_id=1, source_target_pairs={{0,1},{1,0},{2,3},{3,2},{4,5},{5,4},{6,7},{7,6},{8,9},{9,8},{10,11... | collective-permute-start | bytes 221192 | tf_op jit(solution)/shard_map/ppermute | solution.py:795
  8.8 0.0 copy-done.10
  8.8 0.0 copy-done.9
  8.8 0.0 copy-done.8
  8.8 0.0 copy-done.7
  8.8 0.0 copy-done.6
  8.8 0.0 copy-done.5
  8.8 0.0 copy-done.4
  8.8 0.0 copy-done.1
  8.9 4.8 %edge_columns.1 = (f32[12,2,384,128]{3,2,1,0:T(8,128)S(1)}, f32[12,2,384,128]{3,2,1,0:T(8,128)S(1)}, f32[2,384,128]{2,1,0:T(8,128)S(1)}, f32[6,2,408,128]{3,2,1,...) custom-call(s32[384,256]{1,0:T(8,128)S(1)} %copy-done.4, s32[384,256]{1,0:T(8,128)S(1)} %copy-done.5, ...), custom_call_target="tpu_custom_call" | custom-call | flops 5000000 | bytes 12582912 | tf_op jit(solution)/shard_map/edge_columns/pallas_call | solution.py:305
  13.7 0.0 collective-permute-done.refs_0_
  13.7 0.0 collective-permute-done.1.refs_1_
  13.7 0.1 halo_rows.1
  13.9 1.4 %collective-permute-start.2 = (f32[408,128]{1,0:T(8,128)S(1)}, f32[408,128]{1,0:T(8,128)S(1)}, u32[]{:S(2)}, u32[]{:S(2)}) collective-permute-start(f32[408,128]{1,0:T(8,128)S(1)} %get-tuple-element.36.refs_3_), channel_id=1, source_target_pairs={{0,28},{4,8},{8,4},{12,16},{16,12},{20,24},{24,20},{28,0},{1,29},{... | collective-permute-start | bytes 626696 | tf_op jit(solution)/shard_map/ppermute | solution.py:799
  15.3 0.3 collective-permute-start.3
  15.5 6.0 %advect.1 = (f32[12,2,384,128]{3,2,1,0:T(8,128)S(1)}, f32[53,8,384]{2,1,0:T(8,128)S(1)}, f32[53,8,384]{2,1,0:T(8,128)S(1)}, f32[51,8,384]{2,1,0:T(8,128)S(1)}, f...) custom-call(f32[12,2,384,128]{3,2,1,0:T(8,128)S(1)} %get-tuple-eleme, ...), custom_call_target="tpu_custom_call" | custom-call | flops 30000000 | bytes 16777216 | tf_op jit(solution)/shard_map/advect/pallas_call | solution.py:526
  21.5 0.7 %collective-permute-done.2.refs_5_ = f32[408,128]{1,0:T(8,128)S(1)} collective-permute-done((f32[408,128]{1,0:T(8,128)S(1)}, f32[408,128]{1,0:T(8,128)S(1)}, u32[]{:S(2)}, u32[]{:S(2)}) %collective-permute-start.2) | collective-permute-done | bytes 208928 | tf_op jit(solution)/shard_map/ppermute | solution.py:799
  22.2 0.0 collective-permute-done.3.refs_6_
  22.2 9.3 %ice.1 = (f32[6,384,256]{2,1,0:T(8,128)}, f32[6,384,256]{2,1,0:T(8,128)}, f32[384,256]{1,0:T(8,128)}, f32[384,256]{1,0:T(8,128)}) custom-call(f32[6,2,408,128]{3,2,1,0:T(8,128)S(1)} %get-tuple-element.30.refs_4_.refs_0_, f32[12,2,384,128]{3,2,1,0:T(8,128)S(1)} %get-tuple-element.35.refs_1_, f32[12,2,384,128]{3,2,1,0:T(8,128)S(1)} %get-tuple-element.32.refs_1_.refs_2_, ...), custom_call_target="tpu_custom_call" | custom-call | flops 60000000 | bytes 16777216 | tf_op jit(solution)/shard_map/ice/pallas_call | solution.py:754
  (3 shorter events, 0.0 us)
Async XLA Ops:
  0.6 8.2 %copy-start.10 = (f32[384,256]{1,0:T(8,128)S(1)}, f32[384,256]{1,0:T(8,128)}, u32[]{:S(2)}) copy-start(f32[384,256]{1,0:T(8,128)} %refs_6_.3) | copy-start | bytes 1179652
  0.6 8.2 %copy-start.9 = (f32[384,256]{1,0:T(8,128)S(1)}, f32[384,256]{1,0:T(8,128)}, u32[]{:S(2)}) copy-start(f32[384,256]{1,0:T(8,128)} %refs_5_.3) | copy-start | bytes 1179652
  0.7 8.1 %copy-start.8 = (f32[384,256]{1,0:T(8,128)S(1)}, f32[384,256]{1,0:T(8,128)}, u32[]{:S(2)}) copy-start(f32[384,256]{1,0:T(8,128)} %refs_4_.3) | copy-start | bytes 1179652
  0.7 8.1 %copy-start.7 = (f32[384,256]{1,0:T(8,128)S(1)}, f32[384,256]{1,0:T(8,128)}, u32[]{:S(2)}) copy-start(f32[384,256]{1,0:T(8,128)} %refs_3_.3) | copy-start | bytes 1179652
  0.7 8.1 %copy-start.6 = (f32[384,256]{1,0:T(8,128)S(1)}, f32[384,256]{1,0:T(8,128)}, u32[]{:S(2)}) copy-start(f32[384,256]{1,0:T(8,128)} %refs_2_.3) | copy-start | bytes 1179652
  0.7 8.1 %copy-start.5 = (s32[384,256]{1,0:T(8,128)S(1)}, s32[384,256]{1,0:T(8,128)}, u32[]{:S(2)}) copy-start(s32[384,256]{1,0:T(8,128)} %refs_1_.3) | copy-start | bytes 1179652
  0.7 8.1 %copy-start.4 = (s32[384,256]{1,0:T(8,128)S(1)}, s32[384,256]{1,0:T(8,128)}, u32[]{:S(2)}) copy-start(s32[384,256]{1,0:T(8,128)} %refs_0_.3) | copy-start | bytes 1179652
  0.7 8.1 %copy-start.1 = (f32[6,384,256]{2,1,0:T(8,128)S(1)}, f32[6,384,256]{2,1,0:T(8,128)}, u32[]{:S(2)}) copy-start(f32[6,384,256]{2,1,0:T(8,128)} %refs_8_.3) | copy-start | bytes 7077892
  0.7 8.1 %copy-start = (f32[6,384,256]{2,1,0:T(8,128)S(1)}, f32[6,384,256]{2,1,0:T(8,128)}, u32[]{:S(2)}) copy-start(f32[6,384,256]{2,1,0:T(8,128)} %refs_7_.3) | copy-start | bytes 7077892
  0.7 8.1 %copy-start.3 = (f32[6,384,256]{2,1,0:T(8,128)S(1)}, f32[6,384,256]{2,1,0:T(8,128)}, u32[]{:S(2)}) copy-start(f32[6,384,256]{2,1,0:T(8,128)} %refs_10_.3) | copy-start | bytes 7077892
  0.7 8.1 %copy-start.2 = (f32[6,384,256]{2,1,0:T(8,128)S(1)}, f32[6,384,256]{2,1,0:T(8,128)}, u32[]{:S(2)}) copy-start(f32[6,384,256]{2,1,0:T(8,128)} %refs_9_.3) | copy-start | bytes 7077892
  1.9 11.8 %collective-permute-start = (f32[72,256]{1,0:T(8,128)S(1)}, f32[72,256]{1,0:T(8,128)S(1)}, u32[]{:S(2)}, u32[]{:S(2)}) collective-permute-start(f32[72,256]{1,0:T(8,128)S(1)} %get-tuple-element.25), channel_id=1, source_target_pairs={{1,2},{2,1},{3,31},{5,6},{6,5},{7,27},{9,10},{10,9},{11,23},{13,14... | collective-permute-start | bytes 221192 | tf_op jit(solution)/shard_map/ppermute | solution.py:794
  2.8 11.0 %collective-permute-start.1 = (f32[72,256]{1,0:T(8,128)S(1)}, f32[72,256]{1,0:T(8,128)S(1)}, u32[]{:S(2)}, u32[]{:S(2)}) collective-permute-start(f32[72,256]{1,0:T(8,128)S(1)} %get-tuple-element.26), channel_id=1, source_target_pairs={{0,1},{1,0},{2,3},{3,2},{4,5},{5,4},{6,7},{7,6},{8,9},{9,8},{10,11... | collective-permute-start | bytes 221192 | tf_op jit(solution)/shard_map/ppermute | solution.py:795
  13.9 8.3 %collective-permute-start.2 = (f32[408,128]{1,0:T(8,128)S(1)}, f32[408,128]{1,0:T(8,128)S(1)}, u32[]{:S(2)}, u32[]{:S(2)}) collective-permute-start(f32[408,128]{1,0:T(8,128)S(1)} %get-tuple-element.36.refs_3_), channel_id=1, source_target_pairs={{0,28},{4,8},{8,4},{12,16},{16,12},{20,24},{24,20},{28,0},{1,29},{... | collective-permute-start | bytes 626696 | tf_op jit(solution)/shard_map/ppermute | solution.py:799
  15.3 6.9 %collective-permute-start.3 = (f32[408,128]{1,0:T(8,128)S(1)}, f32[408,128]{1,0:T(8,128)S(1)}, u32[]{:S(2)}, u32[]{:S(2)}) collective-permute-start(f32[408,128]{1,0:T(8,128)S(1)} %get-tuple-element.37.refs_4_), channel_id=1, source_target_pairs={{0,4},{4,0},{8,12},{12,8},{16,20},{20,16},{24,28},{28,24},{1,5},{5... | collective-permute-start | bytes 626696 | tf_op jit(solution)/shard_map/ppermute | solution.py:798
where the time goes:
time: 31.6 us; the launch traced here: 31.5 us
  Pallas kernels  21.4 us (68%)
  starting transfers between devices  8.48 us (27%)
  between operations  0.82 us (3%)
  waiting for transfers between devices  0.69 us (2%)
    pallas_call x1, Pallas kernels, ice_and_edges(): pl.pallas_call(lambda *refs: ice_kernel(levels, rows, *refs), in_specs=[V...  9.29 us
    ppermute x1, starting transfers between devices, per_device(): first = lax.ppermute(first, ('lon', 'lat'), first_pairs)  6.04 us
    pallas_call x1, Pallas kernels, advect(): pl.pallas_call(lambda *refs: advect_kernel(levels, row_total, *refs), in_...  5.97 us
    pallas_call x1, Pallas kernels, load_and_pack_columns(): pl.pallas_call(lambda *refs: columns_kernel(levels, *refs), in_specs=[VME...  4.83 us
    ppermute x1, starting transfers between devices, per_device(): inter_in = lax.ppermute(inter, 'lon', inter_pairs)  1.37 us
    pallas_call x1, Pallas kernels, pack_rows(): pl.pallas_call(lambda *refs: rows_kernel(levels, *refs), grid=(1,), in_sp...  1.2 us
    ppermute x1, starting transfers between devices, per_device(): second = lax.ppermute(second, ('lon', 'lat'), second_pairs)  0.8 us
    ppermute x1, waiting for transfers between devices, per_device(): inter_in = lax.ppermute(inter, 'lon', inter_pairs)  0.68 us
  transfers between devices with their start and end apart: 4, of which 1 were waited for; matrix products, arithmetic and copies ran while one was open for 0% of the time, Pallas kernels for 34%

commit v1 on v0

--- a/solution.py
+++ b/solution.py
@@ -120,7 +120,7 @@
 
 def rows_kernel(levels, *refs):
     tops, bottoms = refs[0:12], refs[12:24]
-    second_ref, first_ref = refs[24:26]
+    first_ref, second_ref = refs[24:26]
     even = lax.rem(lax.axis_index("lat"), 2) == 0
 
     def message(group, row, northward):
@@ -317,7 +317,7 @@
     )(*[in_vmem(a) for a in (land, ice, u, v, pressure, wind_x, wind_y, east, north, temp, salt)])
 
 
-def halo_kernel(levels, rows, second, first, field_in, inter_in, intra_in,
+def halo_kernel(levels, rows, first, second, field_in, inter_in, intra_in,
                 halo_ref, field_out, inter_out, intra_out):
     lat = lax.axis_index("lat")
     even = lax.rem(lat, 2) == 0
@@ -354,7 +354,7 @@
         intra_out[at : at + HALO, :] = jnp.where(on_even_lon(), eastward, westward)
 
 
-def merge_halo(second, first, fields, inter_msg, intra_msg, levels, rows):
+def merge_halo(first, second, fields, inter_msg, intra_msg, levels, rows):
     height, cols = first.shape
     return pl.pallas_call(
         lambda *refs: halo_kernel(levels, rows, *refs),
@@ -368,7 +368,7 @@
         name="halo_rows",
         compiler_params=pltpu.CompilerParams(vmem_limit_bytes=8 << 20),
         cost_estimate=pl.CostEstimate(flops=100000, bytes_accessed=1 << 19, transcendentals=0),
-    )(second, first, in_vmem(fields), in_vmem(inter_msg), in_vmem(intra_msg))
+    )(first, second, in_vmem(fields), in_vmem(inter_msg), in_vmem(intra_msg))
 
 
 def advect_kernel(levels, row_total, tracer_ref, speed_ref, sea, halo, field_ref,
@@ -790,11 +790,11 @@
                 second_pairs.append((place(lat, lon), place(((lat + 1) ^ 1) - 1, lon)))
     inter_pairs = [(i, (i - 1 if i % 2 == 0 else i + 1) % lon_count) for i in range(lon_count)]
     intra_pairs = [(i, i ^ 1) for i in range(lon_count)]
-    second, first = pack_rows(arrays, levels, rows, cols, height)
+    first, second = pack_rows(arrays, levels, rows, cols, height)
+    first = lax.ppermute(first, ("lon", "lat"), first_pairs)
     second = lax.ppermute(second, ("lon", "lat"), second_pairs)
-    first = lax.ppermute(first, ("lon", "lat"), first_pairs)
     tracers, speeds, sea, fields, inter, intra = load_and_pack_columns(arrays, levels, rows, cols)
-    halo, fields, inter, intra = merge_halo(second, first, fields, inter, intra, levels, rows)
+    halo, fields, inter, intra = merge_halo(first, second, fields, inter, intra, levels, rows)
     intra_in = lax.ppermute(intra, "lon", intra_pairs)
     inter_in = lax.ppermute(inter, "lon", inter_pairs)
     moved, *state = advect(tracers, speeds, sea, halo, fields, levels, rows * lat_count)

time: 31.6 us -> 30.2 us (0.956)
  the two profiles are of different devices: /device:TPU:0 before, /device:TPU:8 now
where the time goes in v1:
time: 30.2 us; the launch traced here: 30 us
  Pallas kernels  21.4 us (71%)
  starting transfers between devices  7.01 us (23%)
  between operations  0.86 us (3%)
  waiting for transfers between devices  0.69 us (2%)
    pallas_call x1, Pallas kernels, ice_and_edges(): pl.pallas_call(lambda *refs: ice_kernel(levels, rows, *refs), in_specs=[V...  9.29 us
    pallas_call x1, Pallas kernels, advect(): pl.pallas_call(lambda *refs: advect_kernel(levels, row_total, *refs), in_...  5.97 us
    ppermute x1, starting transfers between devices, per_device(): second = lax.ppermute(second, ('lon', 'lat'), second_pairs)  5.3 us
    pallas_call x1, Pallas kernels, load_and_pack_columns(): pl.pallas_call(lambda *refs: columns_kernel(levels, *refs), in_specs=[VME...  4.83 us
    ppermute x1, starting transfers between devices, per_device(): inter_in = lax.ppermute(inter, 'lon', inter_pairs)  1.37 us
    pallas_call x1, Pallas kernels, pack_rows(): pl.pallas_call(lambda *refs: rows_kernel(levels, *refs), grid=(1,), in_sp...  1.2 us
    ppermute x1, waiting for transfers between devices, per_device(): inter_in = lax.ppermute(inter, 'lon', inter_pairs)  0.68 us
  transfers between devices with their start and end apart: 4, of which 1 were waited for; matrix products, arithmetic and copies ran while one was open for 0% of the time, Pallas kernels for 36%

profile of v1, /device:TPU:8, one launch (start us, length us, event | category | flops | bytes accessed | tf_op | source)
XLA Modules:
  0.0 30.0 jit_solution(13964845554256769772)
XLA Ops:
  0.6 0.0 copy-start.10
  0.6 0.0 copy-start.9
  0.7 0.0 copy-start.8
  0.7 0.0 copy-start.7
  0.7 0.0 copy-start.6
  0.7 0.0 copy-start.5
  0.7 0.0 copy-start.4
  0.7 0.0 copy-start.1
  0.7 0.0 copy-start
  0.7 0.0 copy-start.3
  0.7 0.0 copy-start.2
  0.7 1.2 %edge_rows.1 = (f32[72,256]{1,0:T(8,128)S(1)}, f32[72,256]{1,0:T(8,128)S(1)}) custom-call(s32[384,256]{1,0:T(8,128)} %refs_0_.3, s32[384,256]{1,0:T(8,128)} %refs_1_.3, f32[384,256]{1,0:T(8,128)} %refs_2_.3, f32[384,256]{1,0:T(8,128)} %refs_3_.3, f32[384,256]{1,0:T(8,128)} %refs_4_.3, f32[384,256]{1,0:T(8,128)} %refs_5_.3, f32[384,256]{1,0:T(8,128)} %refs_6_.3, ...), custom_call_target="tpu_custom_call" | custom-call | flops 100000 | bytes 1048576 | tf_op jit(solution)/shard_map/edge_rows/pallas_call | solution.py:170
  1.9 0.1 collective-permute-start
  2.0 5.3 %collective-permute-start.1 = (f32[72,256]{1,0:T(8,128)S(1)}, f32[72,256]{1,0:T(8,128)S(1)}, u32[]{:S(2)}, u32[]{:S(2)}) collective-permute-start(f32[72,256]{1,0:T(8,128)S(1)} %get-tuple-element.26), channel_id=1, source_target_pairs={{1,2},{2,1},{3,31},{5,6},{6,5},{7,27},{9,10},{10,9},{11,23},{13,14... | collective-permute-start | bytes 221192 | tf_op jit(solution)/shard_map/ppermute | solution.py:795
  7.3 0.0 copy-done.10
  7.3 0.0 copy-done.9
  7.4 0.0 copy-done.8
  7.4 0.0 copy-done.7
  7.4 0.0 copy-done.6
  7.4 0.0 copy-done.5
  7.4 0.0 copy-done.4
  7.4 0.0 copy-done.1
  7.4 4.8 %edge_columns.1 = (f32[12,2,384,128]{3,2,1,0:T(8,128)S(1)}, f32[12,2,384,128]{3,2,1,0:T(8,128)S(1)}, f32[2,384,128]{2,1,0:T(8,128)S(1)}, f32[6,2,408,128]{3,2,1,...) custom-call(s32[384,256]{1,0:T(8,128)S(1)} %copy-done.4, s32[384,256]{1,0:T(8,128)S(1)} %copy-done.5, ...), custom_call_target="tpu_custom_call" | custom-call | flops 5000000 | bytes 12582912 | tf_op jit(solution)/shard_map/edge_columns/pallas_call | solution.py:305
  12.3 0.0 collective-permute-done.refs_0_
  12.3 0.0 collective-permute-done.1.refs_1_
  12.3 0.1 halo_rows.1
  12.5 1.4 %collective-permute-start.2 = (f32[408,128]{1,0:T(8,128)S(1)}, f32[408,128]{1,0:T(8,128)S(1)}, u32[]{:S(2)}, u32[]{:S(2)}) collective-permute-start(f32[408,128]{1,0:T(8,128)S(1)} %get-tuple-element.36.refs_3_), channel_id=1, source_target_pairs={{0,28},{4,8},{8,4},{12,16},{16,12},{20,24},{24,20},{28,0},{1,29},{... | collective-permute-start | bytes 626696 | tf_op jit(solution)/shard_map/ppermute | solution.py:799
  13.8 0.3 collective-permute-start.3
  14.1 6.0 %advect.1 = (f32[12,2,384,128]{3,2,1,0:T(8,128)S(1)}, f32[53,8,384]{2,1,0:T(8,128)S(1)}, f32[53,8,384]{2,1,0:T(8,128)S(1)}, f32[51,8,384]{2,1,0:T(8,128)S(1)}, f...) custom-call(f32[12,2,384,128]{3,2,1,0:T(8,128)S(1)} %get-tuple-eleme, ...), custom_call_target="tpu_custom_call" | custom-call | flops 30000000 | bytes 16777216 | tf_op jit(solution)/shard_map/advect/pallas_call | solution.py:526
  20.1 0.7 %collective-permute-done.2.refs_5_ = f32[408,128]{1,0:T(8,128)S(1)} collective-permute-done((f32[408,128]{1,0:T(8,128)S(1)}, f32[408,128]{1,0:T(8,128)S(1)}, u32[]{:S(2)}, u32[]{:S(2)}) %collective-permute-start.2) | collective-permute-done | bytes 208928 | tf_op jit(solution)/shard_map/ppermute | solution.py:799
  20.8 0.0 collective-permute-done.3.refs_6_
  20.8 9.3 %ice.1 = (f32[6,384,256]{2,1,0:T(8,128)}, f32[6,384,256]{2,1,0:T(8,128)}, f32[384,256]{1,0:T(8,128)}, f32[384,256]{1,0:T(8,128)}) custom-call(f32[6,2,408,128]{3,2,1,0:T(8,128)S(1)} %get-tuple-element.30.refs_4_.refs_0_, f32[12,2,384,128]{3,2,1,0:T(8,128)S(1)} %get-tuple-element.35.refs_1_, f32[12,2,384,128]{3,2,1,0:T(8,128)S(1)} %get-tuple-element.32.refs_1_.refs_2_, ...), custom_call_target="tpu_custom_call" | custom-call | flops 60000000 | bytes 16777216 | tf_op jit(solution)/shard_map/ice/pallas_call | solution.py:754
  (3 shorter events, 0.0 us)
Async XLA Ops:
  0.6 6.7 %copy-start.10 = (f32[384,256]{1,0:T(8,128)S(1)}, f32[384,256]{1,0:T(8,128)}, u32[]{:S(2)}) copy-start(f32[384,256]{1,0:T(8,128)} %refs_6_.3) | copy-start | bytes 1179652
  0.6 6.7 %copy-start.9 = (f32[384,256]{1,0:T(8,128)S(1)}, f32[384,256]{1,0:T(8,128)}, u32[]{:S(2)}) copy-start(f32[384,256]{1,0:T(8,128)} %refs_5_.3) | copy-start | bytes 1179652
  0.7 6.7 %copy-start.8 = (f32[384,256]{1,0:T(8,128)S(1)}, f32[384,256]{1,0:T(8,128)}, u32[]{:S(2)}) copy-start(f32[384,256]{1,0:T(8,128)} %refs_4_.3) | copy-start | bytes 1179652
  0.7 6.7 %copy-start.7 = (f32[384,256]{1,0:T(8,128)S(1)}, f32[384,256]{1,0:T(8,128)}, u32[]{:S(2)}) copy-start(f32[384,256]{1,0:T(8,128)} %refs_3_.3) | copy-start | bytes 1179652
  0.7 6.7 %copy-start.6 = (f32[384,256]{1,0:T(8,128)S(1)}, f32[384,256]{1,0:T(8,128)}, u32[]{:S(2)}) copy-start(f32[384,256]{1,0:T(8,128)} %refs_2_.3) | copy-start | bytes 1179652
  0.7 6.7 %copy-start.5 = (s32[384,256]{1,0:T(8,128)S(1)}, s32[384,256]{1,0:T(8,128)}, u32[]{:S(2)}) copy-start(s32[384,256]{1,0:T(8,128)} %refs_1_.3) | copy-start | bytes 1179652
  0.7 6.7 %copy-start.4 = (s32[384,256]{1,0:T(8,128)S(1)}, s32[384,256]{1,0:T(8,128)}, u32[]{:S(2)}) copy-start(s32[384,256]{1,0:T(8,128)} %refs_0_.3) | copy-start | bytes 1179652
  0.7 6.7 %copy-start.1 = (f32[6,384,256]{2,1,0:T(8,128)S(1)}, f32[6,384,256]{2,1,0:T(8,128)}, u32[]{:S(2)}) copy-start(f32[6,384,256]{2,1,0:T(8,128)} %refs_8_.3) | copy-start | bytes 7077892
  0.7 6.7 %copy-start = (f32[6,384,256]{2,1,0:T(8,128)S(1)}, f32[6,384,256]{2,1,0:T(8,128)}, u32[]{:S(2)}) copy-start(f32[6,384,256]{2,1,0:T(8,128)} %refs_7_.3) | copy-start | bytes 7077892
  0.7 6.7 %copy-start.3 = (f32[6,384,256]{2,1,0:T(8,128)S(1)}, f32[6,384,256]{2,1,0:T(8,128)}, u32[]{:S(2)}) copy-start(f32[6,384,256]{2,1,0:T(8,128)} %refs_10_.3) | copy-start | bytes 7077892
  0.7 6.7 %copy-start.2 = (f32[6,384,256]{2,1,0:T(8,128)S(1)}, f32[6,384,256]{2,1,0:T(8,128)}, u32[]{:S(2)}) copy-start(f32[6,384,256]{2,1,0:T(8,128)} %refs_9_.3) | copy-start | bytes 7077892
  1.9 10.3 %collective-permute-start = (f32[72,256]{1,0:T(8,128)S(1)}, f32[72,256]{1,0:T(8,128)S(1)}, u32[]{:S(2)}, u32[]{:S(2)}) collective-permute-start(f32[72,256]{1,0:T(8,128)S(1)} %get-tuple-element.25), channel_id=1, source_target_pairs={{0,1},{1,0},{2,3},{3,2},{4,5},{5,4},{6,7},{7,6},{8,9},{9,8},{10,11... | collective-permute-start | bytes 221192 | tf_op jit(solution)/shard_map/ppermute | solution.py:794
  2.0 10.3 %collective-permute-start.1 = (f32[72,256]{1,0:T(8,128)S(1)}, f32[72,256]{1,0:T(8,128)S(1)}, u32[]{:S(2)}, u32[]{:S(2)}) collective-permute-start(f32[72,256]{1,0:T(8,128)S(1)} %get-tuple-element.26), channel_id=1, source_target_pairs={{1,2},{2,1},{3,31},{5,6},{6,5},{7,27},{9,10},{10,9},{11,23},{13,14... | collective-permute-start | bytes 221192 | tf_op jit(solution)/shard_map/ppermute | solution.py:795
  12.5 8.3 %collective-permute-start.2 = (f32[408,128]{1,0:T(8,128)S(1)}, f32[408,128]{1,0:T(8,128)S(1)}, u32[]{:S(2)}, u32[]{:S(2)}) collective-permute-start(f32[408,128]{1,0:T(8,128)S(1)} %get-tuple-element.36.refs_3_), channel_id=1, source_target_pairs={{0,28},{4,8},{8,4},{12,16},{16,12},{20,24},{24,20},{28,0},{1,29},{... | collective-permute-start | bytes 626696 | tf_op jit(solution)/shard_map/ppermute | solution.py:799
  13.8 6.9 %collective-permute-start.3 = (f32[408,128]{1,0:T(8,128)S(1)}, f32[408,128]{1,0:T(8,128)S(1)}, u32[]{:S(2)}, u32[]{:S(2)}) collective-permute-start(f32[408,128]{1,0:T(8,128)S(1)} %get-tuple-element.37.refs_4_), channel_id=1, source_target_pairs={{0,4},{4,0},{8,12},{12,8},{16,20},{20,16},{24,28},{28,24},{1,5},{5... | collective-permute-start | bytes 626696 | tf_op jit(solution)/shard_map/ppermute | solution.py:798

commit v2 on v1

--- a/solution.py
+++ b/solution.py
@@ -542,7 +542,7 @@
      base_u, base_v, third, force, push_x, push_y, turn_a, turn_b,
      temp_out, salt_out, u_out, v_out,
      moved, done, vel_u, vel_v, str_a, str_b, str_c,
-     third_x, force_x, push_x_x, push_y_x, edges,
+     third_x, force_x, push_x_x, push_y_x, edges, diff_u, diff_v,
      out_sem, vel_sem) = refs
     tiles = tracers_in.shape[1]
     count = sublane_rows(rows)
@@ -574,6 +574,9 @@
         flux = turn(edges[put, :], -(TRACER_LANE + 2 * f))
         low = tracers_in[f, 0, put, :] + jnp.where(lane == 0, flux, 0.0)
         return low, tracers_in[f, tiles - 1, put, :] - jnp.where(lane == LANES - 1, flux, 0.0)
+
+    unused = ((lane >= 16) & (lane < 32)) | ((lane >= 64) & (lane < 88))
+    unused = unused | ((lane >= 112) & (lane < 120))
 
     def insert(i):
         west, east_side = sides(spread(inter_in, i, count), spread(intra_in, i, count))
@@ -589,9 +592,11 @@
             x = jnp.where((lane >= start) & (lane < start + HALO), west, east_side)
             beyond.append(turn(x, 104 - HALO * f))
         beyond[2] = beyond[2] * beyond[3] * (1.0 / 12.0)
-        for x, (source, target, shift, t, factor) in zip(beyond, targets):
+        for f_index, (x, (source, target, shift, t, factor)) in enumerate(zip(beyond, targets)):
             x = x if factor == 1.0 else x * factor
             x = jnp.where(lane >= 104, x, source[i + shift, :, cut(tiles)])
+            if f_index in (2, 3):
+                x = jnp.where(unused, 0.0, x)
             writes.append((target, (i + shift, whole, cut(t)), x))
         own_lanes = slice(0, LANES * tiles)
         for source, target in ((base_u, vel_u), (base_v, vel_v)):
@@ -634,12 +639,26 @@
             for t in range(tiles)
         ]
 
+    def lane_difference(source, target):
+        k = lax.broadcasted_iota(jnp.int32, (2 * LANES, LANES), 0) % LANES
+        x = lax.broadcasted_iota(jnp.int32, (2 * LANES, LANES), 1)
+        after = jnp.where(k == (x + 1) % LANES, 1.0, 0.0)
+        matrix = (after - jnp.where(k == (x + LANES - 1) % LANES, 1.0, 0.0)).astype(jnp.bfloat16)
+        for t in range(wide):
+            f = source[1 : count + 2, :, cut(t)].reshape((count + 1) * SUBLANES, LANES)
+            high = f.astype(jnp.bfloat16)
+            rest = (f - high.astype(F32)).astype(jnp.bfloat16)
+            parts = jnp.concatenate([high, rest], axis=1)
+            result = jnp.dot(parts, matrix, preferred_element_type=F32)
+            target[:, :, cut(t)] = result.reshape(count + 1, SUBLANES, LANES)
+
     def strain_stress(step):
         seen = {}
+        lane_difference(vel_u, diff_u)
+        lane_difference(vel_v, diff_v)
         for i in range(count):
             for t in range(wide):
-                u, v = (load_once(r, n, seen, i + 1, t) for n, r in enumerate((vel_u, vel_v)))
-                dudx, dvdx = turn(u, -1) - turn(u, 1), turn(v, -1) - turn(v, 1)
+                dudx, dvdx = diff_u[i, :, cut(t)], diff_v[i, :, cut(t)]
                 dudy, dvdy = (
                     load_once(r, n, seen, i + 2, t) - load_once(r, n, seen, i, t)
                     for n, r in enumerate((vel_u, vel_v))
@@ -651,11 +670,10 @@
                 quarter = 0.25 * zeta
                 even = zeta * div - base
                 odd = quarter * ten
-                keep = constant(third, third_x, i, t)
                 for ref, new in (
                     (str_a, even + odd), (str_b, even - odd), (str_c, quarter * shr)
                 ):
-                    ref[i + 1, :, cut(t)] = new + keep * ref[i + 1, :, cut(t)]
+                    ref[i + 1, :, cut(t)] = new + (1.0 / 3.0) * ref[i + 1, :, cut(t)]
             fix(step, i)
         wrap(str_b, count)
         wrap(str_c, count)
@@ -751,6 +769,7 @@
     flat = jax.ShapeDtypeStruct((rows, cols), F32)
     looped = pltpu.VMEM((count + 2, SUBLANES, LANES * (tiles + 1)), F32)
     narrow = pltpu.VMEM((count, SUBLANES, LANES), F32)
+    difference = pltpu.VMEM((count + 1, SUBLANES, LANES * (tiles + 1)), F32)
     return pl.pallas_call(
         lambda *refs: ice_kernel(levels, rows, *refs),
         in_specs=[VMEM_SPEC] * len(operands),
@@ -761,6 +780,7 @@
             pltpu.VMEM((2, tiles, count * SUBLANES, LANES), F32),
             looped, looped, looped, looped, looped,
             narrow, narrow, narrow, narrow, pltpu.VMEM((rows, LANES), F32),
+            difference, difference,
             pltpu.SemaphoreType.DMA((SUBCYCLES + 1, 2, tiles)),
             pltpu.SemaphoreType.DMA((2, tiles)),
         ],

time: 30.2 us -> 30.6 us (1.013)
  Pallas kernels: 21.4 us -> 21.9 us
    pallas_call x1, Pallas kernels: 9.29 us -> 9.73 us  [ice_and_edges(): pl.pallas_call(lambda *refs: ice_kernel(levels, rows, *refs), in_specs=[V...]
  transfers between devices with their start and end apart: 4 -> 4, of which waited for: 1 -> 1; matrix products, arithmetic and copies ran while one was open for 0% -> 0% of each run, Pallas kernels for 36% -> 35%
where the time goes in v2:
time: 30.6 us; the launch traced here: 30.5 us
  Pallas kernels  21.9 us (72%)
  starting transfers between devices  7.01 us (23%)
  between operations  0.86 us (3%)
  waiting for transfers between devices  0.69 us (2%)
    pallas_call x1, Pallas kernels, ice_and_edges(): pl.pallas_call(lambda *refs: ice_kernel(levels, rows, *refs), in_specs=[V...  9.73 us
    pallas_call x1, Pallas kernels, advect(): pl.pallas_call(lambda *refs: advect_kernel(levels, row_total, *refs), in_...  5.97 us
    ppermute x1, starting transfers between devices, per_device(): second = lax.ppermute(second, ('lon', 'lat'), second_pairs)  5.3 us
    pallas_call x1, Pallas kernels, load_and_pack_columns(): pl.pallas_call(lambda *refs: columns_kernel(levels, *refs), in_specs=[VME...  4.83 us
    ppermute x1, starting transfers between devices, per_device(): inter_in = lax.ppermute(inter, 'lon', inter_pairs)  1.37 us
    pallas_call x1, Pallas kernels, pack_rows(): pl.pallas_call(lambda *refs: rows_kernel(levels, *refs), grid=(1,), in_sp...  1.2 us
    ppermute x1, waiting for transfers between devices, per_device(): inter_in = lax.ppermute(inter, 'lon', inter_pairs)  0.68 us
  transfers between devices with their start and end apart: 4, of which 1 were waited for; matrix products, arithmetic and copies ran while one was open for 0% of the time, Pallas kernels for 35%

profile of v2, /device:TPU:8, one launch (start us, length us, event | category | flops | bytes accessed | tf_op | source)
XLA Modules:
  0.0 30.5 jit_solution(16932152473280523702)
XLA Ops:
  0.6 0.0 copy-start.10
  0.6 0.0 copy-start.9
  0.7 0.0 copy-start.8
  0.7 0.0 copy-start.7
  0.7 0.0 copy-start.6
  0.7 0.0 copy-start.5
  0.7 0.0 copy-start.4
  0.7 0.0 copy-start.1
  0.7 0.0 copy-start
  0.7 0.0 copy-start.3
  0.7 0.0 copy-start.2
  0.7 1.2 %edge_rows.1 = (f32[72,256]{1,0:T(8,128)S(1)}, f32[72,256]{1,0:T(8,128)S(1)}) custom-call(s32[384,256]{1,0:T(8,128)} %refs_0_.3, s32[384,256]{1,0:T(8,128)} %refs_1_.3, f32[384,256]{1,0:T(8,128)} %refs_2_.3, f32[384,256]{1,0:T(8,128)} %refs_3_.3, f32[384,256]{1,0:T(8,128)} %refs_4_.3, f32[384,256]{1,0:T(8,128)} %refs_5_.3, f32[384,256]{1,0:T(8,128)} %refs_6_.3, ...), custom_call_target="tpu_custom_call" | custom-call | flops 100000 | bytes 1048576 | tf_op jit(solution)/shard_map/edge_rows/pallas_call | solution.py:170
  1.9 0.1 collective-permute-start
  2.0 5.3 %collective-permute-start.1 = (f32[72,256]{1,0:T(8,128)S(1)}, f32[72,256]{1,0:T(8,128)S(1)}, u32[]{:S(2)}, u32[]{:S(2)}) collective-permute-start(f32[72,256]{1,0:T(8,128)S(1)} %get-tuple-element.26), channel_id=1, source_target_pairs={{1,2},{2,1},{3,31},{5,6},{6,5},{7,27},{9,10},{10,9},{11,23},{13,14... | collective-permute-start | bytes 221192 | tf_op jit(solution)/shard_map/ppermute | solution.py:815
  7.3 0.0 copy-done.10
  7.3 0.0 copy-done.9
  7.4 0.0 copy-done.8
  7.4 0.0 copy-done.7
  7.4 0.0 copy-done.6
  7.4 0.0 copy-done.5
  7.4 0.0 copy-done.4
  7.4 0.0 copy-done.1
  7.4 4.8 %edge_columns.1 = (f32[12,2,384,128]{3,2,1,0:T(8,128)S(1)}, f32[12,2,384,128]{3,2,1,0:T(8,128)S(1)}, f32[2,384,128]{2,1,0:T(8,128)S(1)}, f32[6,2,408,128]{3,2,1,...) custom-call(s32[384,256]{1,0:T(8,128)S(1)} %copy-done.4, s32[384,256]{1,0:T(8,128)S(1)} %copy-done.5, ...), custom_call_target="tpu_custom_call" | custom-call | flops 5000000 | bytes 12582912 | tf_op jit(solution)/shard_map/edge_columns/pallas_call | solution.py:305
  12.3 0.0 collective-permute-done.refs_0_
  12.3 0.0 collective-permute-done.1.refs_1_
  12.3 0.1 halo_rows.1
  12.5 1.4 %collective-permute-start.2 = (f32[408,128]{1,0:T(8,128)S(1)}, f32[408,128]{1,0:T(8,128)S(1)}, u32[]{:S(2)}, u32[]{:S(2)}) collective-permute-start(f32[408,128]{1,0:T(8,128)S(1)} %get-tuple-element.36.refs_3_), channel_id=1, source_target_pairs={{0,28},{4,8},{8,4},{12,16},{16,12},{20,24},{24,20},{28,0},{1,29},{... | collective-permute-start | bytes 626696 | tf_op jit(solution)/shard_map/ppermute | solution.py:819
  13.8 0.3 collective-permute-start.3
  14.1 6.0 %advect.1 = (f32[12,2,384,128]{3,2,1,0:T(8,128)S(1)}, f32[53,8,384]{2,1,0:T(8,128)S(1)}, f32[53,8,384]{2,1,0:T(8,128)S(1)}, f32[51,8,384]{2,1,0:T(8,128)S(1)}, f...) custom-call(f32[12,2,384,128]{3,2,1,0:T(8,128)S(1)} %get-tuple-eleme, ...), custom_call_target="tpu_custom_call" | custom-call | flops 30000000 | bytes 16777216 | tf_op jit(solution)/shard_map/advect/pallas_call | solution.py:526
  20.1 0.7 %collective-permute-done.2.refs_5_ = f32[408,128]{1,0:T(8,128)S(1)} collective-permute-done((f32[408,128]{1,0:T(8,128)S(1)}, f32[408,128]{1,0:T(8,128)S(1)}, u32[]{:S(2)}, u32[]{:S(2)}) %collective-permute-start.2) | collective-permute-done | bytes 208928 | tf_op jit(solution)/shard_map/ppermute | solution.py:819
  20.8 0.0 collective-permute-done.3.refs_6_
  20.8 9.7 %ice.1 = (f32[6,384,256]{2,1,0:T(8,128)}, f32[6,384,256]{2,1,0:T(8,128)}, f32[384,256]{1,0:T(8,128)}, f32[384,256]{1,0:T(8,128)}) custom-call(f32[6,2,408,128]{3,2,1,0:T(8,128)S(1)} %get-tuple-element.30.refs_4_.refs_0_, f32[12,2,384,128]{3,2,1,0:T(8,128)S(1)} %get-tuple-element.35.refs_1_, f32[12,2,384,128]{3,2,1,0:T(8,128)S(1)} %get-tuple-element.32.refs_1_.refs_2_, ...), custom_call_target="tpu_custom_call" | custom-call | flops 60000000 | bytes 16777216 | tf_op jit(solution)/shard_map/ice/pallas_call | solution.py:773
  (3 shorter events, 0.0 us)
Async XLA Ops:
  0.6 6.7 %copy-start.10 = (f32[384,256]{1,0:T(8,128)S(1)}, f32[384,256]{1,0:T(8,128)}, u32[]{:S(2)}) copy-start(f32[384,256]{1,0:T(8,128)} %refs_6_.3) | copy-start | bytes 1179652
  0.6 6.7 %copy-start.9 = (f32[384,256]{1,0:T(8,128)S(1)}, f32[384,256]{1,0:T(8,128)}, u32[]{:S(2)}) copy-start(f32[384,256]{1,0:T(8,128)} %refs_5_.3) | copy-start | bytes 1179652
  0.7 6.7 %copy-start.8 = (f32[384,256]{1,0:T(8,128)S(1)}, f32[384,256]{1,0:T(8,128)}, u32[]{:S(2)}) copy-start(f32[384,256]{1,0:T(8,128)} %refs_4_.3) | copy-start | bytes 1179652
  0.7 6.7 %copy-start.7 = (f32[384,256]{1,0:T(8,128)S(1)}, f32[384,256]{1,0:T(8,128)}, u32[]{:S(2)}) copy-start(f32[384,256]{1,0:T(8,128)} %refs_3_.3) | copy-start | bytes 1179652
  0.7 6.7 %copy-start.6 = (f32[384,256]{1,0:T(8,128)S(1)}, f32[384,256]{1,0:T(8,128)}, u32[]{:S(2)}) copy-start(f32[384,256]{1,0:T(8,128)} %refs_2_.3) | copy-start | bytes 1179652
  0.7 6.7 %copy-start.5 = (s32[384,256]{1,0:T(8,128)S(1)}, s32[384,256]{1,0:T(8,128)}, u32[]{:S(2)}) copy-start(s32[384,256]{1,0:T(8,128)} %refs_1_.3) | copy-start | bytes 1179652
  0.7 6.7 %copy-start.4 = (s32[384,256]{1,0:T(8,128)S(1)}, s32[384,256]{1,0:T(8,128)}, u32[]{:S(2)}) copy-start(s32[384,256]{1,0:T(8,128)} %refs_0_.3) | copy-start | bytes 1179652
  0.7 6.7 %copy-start.1 = (f32[6,384,256]{2,1,0:T(8,128)S(1)}, f32[6,384,256]{2,1,0:T(8,128)}, u32[]{:S(2)}) copy-start(f32[6,384,256]{2,1,0:T(8,128)} %refs_8_.3) | copy-start | bytes 7077892
  0.7 6.7 %copy-start = (f32[6,384,256]{2,1,0:T(8,128)S(1)}, f32[6,384,256]{2,1,0:T(8,128)}, u32[]{:S(2)}) copy-start(f32[6,384,256]{2,1,0:T(8,128)} %refs_7_.3) | copy-start | bytes 7077892
  0.7 6.7 %copy-start.3 = (f32[6,384,256]{2,1,0:T(8,128)S(1)}, f32[6,384,256]{2,1,0:T(8,128)}, u32[]{:S(2)}) copy-start(f32[6,384,256]{2,1,0:T(8,128)} %refs_10_.3) | copy-start | bytes 7077892
  0.7 6.7 %copy-start.2 = (f32[6,384,256]{2,1,0:T(8,128)S(1)}, f32[6,384,256]{2,1,0:T(8,128)}, u32[]{:S(2)}) copy-start(f32[6,384,256]{2,1,0:T(8,128)} %refs_9_.3) | copy-start | bytes 7077892
  1.9 10.3 %collective-permute-start = (f32[72,256]{1,0:T(8,128)S(1)}, f32[72,256]{1,0:T(8,128)S(1)}, u32[]{:S(2)}, u32[]{:S(2)}) collective-permute-start(f32[72,256]{1,0:T(8,128)S(1)} %get-tuple-element.25), channel_id=1, source_target_pairs={{0,1},{1,0},{2,3},{3,2},{4,5},{5,4},{6,7},{7,6},{8,9},{9,8},{10,11... | collective-permute-start | bytes 221192 | tf_op jit(solution)/shard_map/ppermute | solution.py:814
  2.0 10.3 %collective-permute-start.1 = (f32[72,256]{1,0:T(8,128)S(1)}, f32[72,256]{1,0:T(8,128)S(1)}, u32[]{:S(2)}, u32[]{:S(2)}) collective-permute-start(f32[72,256]{1,0:T(8,128)S(1)} %get-tuple-element.26), channel_id=1, source_target_pairs={{1,2},{2,1},{3,31},{5,6},{6,5},{7,27},{9,10},{10,9},{11,23},{13,14... | collective-permute-start | bytes 221192 | tf_op jit(solution)/shard_map/ppermute | solution.py:815
  12.5 8.3 %collective-permute-start.2 = (f32[408,128]{1,0:T(8,128)S(1)}, f32[408,128]{1,0:T(8,128)S(1)}, u32[]{:S(2)}, u32[]{:S(2)}) collective-permute-start(f32[408,128]{1,0:T(8,128)S(1)} %get-tuple-element.36.refs_3_), channel_id=1, source_target_pairs={{0,28},{4,8},{8,4},{12,16},{16,12},{20,24},{24,20},{28,0},{1,29},{... | collective-permute-start | bytes 626696 | tf_op jit(solution)/shard_map/ppermute | solution.py:819
  13.8 6.9 %collective-permute-start.3 = (f32[408,128]{1,0:T(8,128)S(1)}, f32[408,128]{1,0:T(8,128)S(1)}, u32[]{:S(2)}, u32[]{:S(2)}) collective-permute-start(f32[408,128]{1,0:T(8,128)S(1)} %get-tuple-element.37.refs_4_), channel_id=1, source_target_pairs={{0,4},{4,0},{8,12},{12,8},{16,20},{20,16},{24,28},{28,24},{1,5},{5... | collective-permute-start | bytes 626696 | tf_op jit(solution)/shard_map/ppermute | solution.py:818

commit v3 on v1

--- a/solution.py
+++ b/solution.py
@@ -651,11 +651,10 @@
                 quarter = 0.25 * zeta
                 even = zeta * div - base
                 odd = quarter * ten
-                keep = constant(third, third_x, i, t)
                 for ref, new in (
                     (str_a, even + odd), (str_b, even - odd), (str_c, quarter * shr)
                 ):
-                    ref[i + 1, :, cut(t)] = new + keep * ref[i + 1, :, cut(t)]
+                    ref[i + 1, :, cut(t)] = new + (1.0 / 3.0) * ref[i + 1, :, cut(t)]
             fix(step, i)
         wrap(str_b, count)
         wrap(str_c, count)
@@ -727,17 +726,20 @@
             writes.append((moved, (levels, t, put, whole), sss - SALT_RATE * heat))
         return writes
 
-    straight(rows // SUBLANES, warm, 6, 24)
-    for n, out in enumerate((temp_out, salt_out)):
-        for t in range(tiles):
-            finals.append(
-                pltpu.make_async_copy(
-                    moved.at[levels * n, t],
-                    out.at[0, :, pl.ds(LANES * t, LANES)],
-                    out_sem.at[SUBCYCLES, n, t],
+    half = rows // SUBLANES // 2
+    for h in range(2):
+        straight(half, lambda k: warm(half * h + k), 6, half)
+        part = pl.ds(half * h * SUBLANES, half * SUBLANES)
+        for n, out in enumerate((temp_out, salt_out)):
+            for t in range(tiles):
+                finals.append(
+                    pltpu.make_async_copy(
+                        moved.at[levels * n, t, part, :],
+                        out.at[0, part, pl.ds(LANES * t, LANES)],
+                        out_sem.at[SUBCYCLES + h, n, t],
+                    )
                 )
-            )
-            finals[-1].start()
+                finals[-1].start()
     for step in range(SUBCYCLES):
         finals += fixed_rows(step)
     for copy in finals:
@@ -761,7 +763,7 @@
             pltpu.VMEM((2, tiles, count * SUBLANES, LANES), F32),
             looped, looped, looped, looped, looped,
             narrow, narrow, narrow, narrow, pltpu.VMEM((rows, LANES), F32),
-            pltpu.SemaphoreType.DMA((SUBCYCLES + 1, 2, tiles)),
+            pltpu.SemaphoreType.DMA((SUBCYCLES + 2, 2, tiles)),
             pltpu.SemaphoreType.DMA((2, tiles)),
         ],
         name="ice",

time: 30.2 us -> 30.3 us (level)
  no operation moved by 1% of the time
where the time goes in v3:
time: 30.3 us; the launch traced here: 30.2 us
  Pallas kernels  21.6 us (71%)
  starting transfers between devices  7.01 us (23%)
  between operations  0.86 us (3%)
  waiting for transfers between devices  0.69 us (2%)
    pallas_call x1, Pallas kernels, ice_and_edges(): pl.pallas_call(lambda *refs: ice_kernel(levels, rows, *refs), in_specs=[V...  9.41 us
    pallas_call x1, Pallas kernels, advect(): pl.pallas_call(lambda *refs: advect_kernel(levels, row_total, *refs), in_...  5.97 us
    ppermute x1, starting transfers between devices, per_device(): second = lax.ppermute(second, ('lon', 'lat'), second_pairs)  5.3 us
    pallas_call x1, Pallas kernels, load_and_pack_columns(): pl.pallas_call(lambda *refs: columns_kernel(levels, *refs), in_specs=[VME...  4.83 us
    ppermute x1, starting transfers between devices, per_device(): inter_in = lax.ppermute(inter, 'lon', inter_pairs)  1.37 us
    pallas_call x1, Pallas kernels, pack_rows(): pl.pallas_call(lambda *refs: rows_kernel(levels, *refs), grid=(1,), in_sp...  1.2 us
    ppermute x1, waiting for transfers between devices, per_device(): inter_in = lax.ppermute(inter, 'lon', inter_pairs)  0.68 us
  transfers between devices with their start and end apart: 4, of which 1 were waited for; matrix products, arithmetic and copies ran while one was open for 0% of the time, Pallas kernels for 36%

profile of v3, /device:TPU:8, one launch (start us, length us, event | category | flops | bytes accessed | tf_op | source)
XLA Modules:
  0.0 30.2 jit_solution(17684362067491352772)
XLA Ops:
  0.6 0.0 copy-start.10
  0.6 0.0 copy-start.9
  0.7 0.0 copy-start.8
  0.7 0.0 copy-start.7
  0.7 0.0 copy-start.6
  0.7 0.0 copy-start.5
  0.7 0.0 copy-start.4
  0.7 0.0 copy-start.1
  0.7 0.0 copy-start
  0.7 0.0 copy-start.3
  0.7 0.0 copy-start.2
  0.7 1.2 %edge_rows.1 = (f32[72,256]{1,0:T(8,128)S(1)}, f32[72,256]{1,0:T(8,128)S(1)}) custom-call(s32[384,256]{1,0:T(8,128)} %refs_0_.3, s32[384,256]{1,0:T(8,128)} %refs_1_.3, f32[384,256]{1,0:T(8,128)} %refs_2_.3, f32[384,256]{1,0:T(8,128)} %refs_3_.3, f32[384,256]{1,0:T(8,128)} %refs_4_.3, f32[384,256]{1,0:T(8,128)} %refs_5_.3, f32[384,256]{1,0:T(8,128)} %refs_6_.3, ...), custom_call_target="tpu_custom_call" | custom-call | flops 100000 | bytes 1048576 | tf_op jit(solution)/shard_map/edge_rows/pallas_call | solution.py:170
  1.9 0.1 collective-permute-start
  2.0 5.3 %collective-permute-start.1 = (f32[72,256]{1,0:T(8,128)S(1)}, f32[72,256]{1,0:T(8,128)S(1)}, u32[]{:S(2)}, u32[]{:S(2)}) collective-permute-start(f32[72,256]{1,0:T(8,128)S(1)} %get-tuple-element.26), channel_id=1, source_target_pairs={{1,2},{2,1},{3,31},{5,6},{6,5},{7,27},{9,10},{10,9},{11,23},{13,14... | collective-permute-start | bytes 221192 | tf_op jit(solution)/shard_map/ppermute | solution.py:797
  7.3 0.0 copy-done.10
  7.3 0.0 copy-done.9
  7.4 0.0 copy-done.8
  7.4 0.0 copy-done.7
  7.4 0.0 copy-done.6
  7.4 0.0 copy-done.5
  7.4 0.0 copy-done.4
  7.4 0.0 copy-done.1
  7.4 4.8 %edge_columns.1 = (f32[12,2,384,128]{3,2,1,0:T(8,128)S(1)}, f32[12,2,384,128]{3,2,1,0:T(8,128)S(1)}, f32[2,384,128]{2,1,0:T(8,128)S(1)}, f32[6,2,408,128]{3,2,1,...) custom-call(s32[384,256]{1,0:T(8,128)S(1)} %copy-done.4, s32[384,256]{1,0:T(8,128)S(1)} %copy-done.5, ...), custom_call_target="tpu_custom_call" | custom-call | flops 5000000 | bytes 12582912 | tf_op jit(solution)/shard_map/edge_columns/pallas_call | solution.py:305
  12.3 0.0 collective-permute-done.refs_0_
  12.3 0.0 collective-permute-done.1.refs_1_
  12.3 0.1 halo_rows.1
  12.5 1.4 %collective-permute-start.2 = (f32[408,128]{1,0:T(8,128)S(1)}, f32[408,128]{1,0:T(8,128)S(1)}, u32[]{:S(2)}, u32[]{:S(2)}) collective-permute-start(f32[408,128]{1,0:T(8,128)S(1)} %get-tuple-element.36.refs_3_), channel_id=1, source_target_pairs={{0,28},{4,8},{8,4},{12,16},{16,12},{20,24},{24,20},{28,0},{1,29},{... | collective-permute-start | bytes 626696 | tf_op jit(solution)/shard_map/ppermute | solution.py:801
  13.8 0.3 collective-permute-start.3
  14.1 6.0 %advect.1 = (f32[12,2,384,128]{3,2,1,0:T(8,128)S(1)}, f32[53,8,384]{2,1,0:T(8,128)S(1)}, f32[53,8,384]{2,1,0:T(8,128)S(1)}, f32[51,8,384]{2,1,0:T(8,128)S(1)}, f...) custom-call(f32[12,2,384,128]{3,2,1,0:T(8,128)S(1)} %get-tuple-eleme, ...), custom_call_target="tpu_custom_call" | custom-call | flops 30000000 | bytes 16777216 | tf_op jit(solution)/shard_map/advect/pallas_call | solution.py:526
  20.1 0.7 %collective-permute-done.2.refs_5_ = f32[408,128]{1,0:T(8,128)S(1)} collective-permute-done((f32[408,128]{1,0:T(8,128)S(1)}, f32[408,128]{1,0:T(8,128)S(1)}, u32[]{:S(2)}, u32[]{:S(2)}) %collective-permute-start.2) | collective-permute-done | bytes 208928 | tf_op jit(solution)/shard_map/ppermute | solution.py:801
  20.8 0.0 collective-permute-done.3.refs_6_
  20.8 9.4 %ice.1 = (f32[6,384,256]{2,1,0:T(8,128)}, f32[6,384,256]{2,1,0:T(8,128)}, f32[384,256]{1,0:T(8,128)}, f32[384,256]{1,0:T(8,128)}) custom-call(f32[6,2,408,128]{3,2,1,0:T(8,128)S(1)} %get-tuple-element.30.refs_4_.refs_0_, f32[12,2,384,128]{3,2,1,0:T(8,128)S(1)} %get-tuple-element.35.refs_1_, f32[12,2,384,128]{3,2,1,0:T(8,128)S(1)} %get-tuple-element.32.refs_1_.refs_2_, ...), custom_call_target="tpu_custom_call" | custom-call | flops 60000000 | bytes 16777216 | tf_op jit(solution)/shard_map/ice/pallas_call | solution.py:756
  (3 shorter events, 0.0 us)
Async XLA Ops:
  0.6 6.7 %copy-start.10 = (f32[384,256]{1,0:T(8,128)S(1)}, f32[384,256]{1,0:T(8,128)}, u32[]{:S(2)}) copy-start(f32[384,256]{1,0:T(8,128)} %refs_6_.3) | copy-start | bytes 1179652
  0.6 6.7 %copy-start.9 = (f32[384,256]{1,0:T(8,128)S(1)}, f32[384,256]{1,0:T(8,128)}, u32[]{:S(2)}) copy-start(f32[384,256]{1,0:T(8,128)} %refs_5_.3) | copy-start | bytes 1179652
  0.7 6.7 %copy-start.8 = (f32[384,256]{1,0:T(8,128)S(1)}, f32[384,256]{1,0:T(8,128)}, u32[]{:S(2)}) copy-start(f32[384,256]{1,0:T(8,128)} %refs_4_.3) | copy-start | bytes 1179652
  0.7 6.7 %copy-start.7 = (f32[384,256]{1,0:T(8,128)S(1)}, f32[384,256]{1,0:T(8,128)}, u32[]{:S(2)}) copy-start(f32[384,256]{1,0:T(8,128)} %refs_3_.3) | copy-start | bytes 1179652
  0.7 6.7 %copy-start.6 = (f32[384,256]{1,0:T(8,128)S(1)}, f32[384,256]{1,0:T(8,128)}, u32[]{:S(2)}) copy-start(f32[384,256]{1,0:T(8,128)} %refs_2_.3) | copy-start | bytes 1179652
  0.7 6.7 %copy-start.5 = (s32[384,256]{1,0:T(8,128)S(1)}, s32[384,256]{1,0:T(8,128)}, u32[]{:S(2)}) copy-start(s32[384,256]{1,0:T(8,128)} %refs_1_.3) | copy-start | bytes 1179652
  0.7 6.7 %copy-start.4 = (s32[384,256]{1,0:T(8,128)S(1)}, s32[384,256]{1,0:T(8,128)}, u32[]{:S(2)}) copy-start(s32[384,256]{1,0:T(8,128)} %refs_0_.3) | copy-start | bytes 1179652
  0.7 6.7 %copy-start.1 = (f32[6,384,256]{2,1,0:T(8,128)S(1)}, f32[6,384,256]{2,1,0:T(8,128)}, u32[]{:S(2)}) copy-start(f32[6,384,256]{2,1,0:T(8,128)} %refs_8_.3) | copy-start | bytes 7077892
  0.7 6.7 %copy-start = (f32[6,384,256]{2,1,0:T(8,128)S(1)}, f32[6,384,256]{2,1,0:T(8,128)}, u32[]{:S(2)}) copy-start(f32[6,384,256]{2,1,0:T(8,128)} %refs_7_.3) | copy-start | bytes 7077892
  0.7 6.7 %copy-start.3 = (f32[6,384,256]{2,1,0:T(8,128)S(1)}, f32[6,384,256]{2,1,0:T(8,128)}, u32[]{:S(2)}) copy-start(f32[6,384,256]{2,1,0:T(8,128)} %refs_10_.3) | copy-start | bytes 7077892
  0.7 6.7 %copy-start.2 = (f32[6,384,256]{2,1,0:T(8,128)S(1)}, f32[6,384,256]{2,1,0:T(8,128)}, u32[]{:S(2)}) copy-start(f32[6,384,256]{2,1,0:T(8,128)} %refs_9_.3) | copy-start | bytes 7077892
  1.9 10.3 %collective-permute-start = (f32[72,256]{1,0:T(8,128)S(1)}, f32[72,256]{1,0:T(8,128)S(1)}, u32[]{:S(2)}, u32[]{:S(2)}) collective-permute-start(f32[72,256]{1,0:T(8,128)S(1)} %get-tuple-element.25), channel_id=1, source_target_pairs={{0,1},{1,0},{2,3},{3,2},{4,5},{5,4},{6,7},{7,6},{8,9},{9,8},{10,11... | collective-permute-start | bytes 221192 | tf_op jit(solution)/shard_map/ppermute | solution.py:796
  2.0 10.3 %collective-permute-start.1 = (f32[72,256]{1,0:T(8,128)S(1)}, f32[72,256]{1,0:T(8,128)S(1)}, u32[]{:S(2)}, u32[]{:S(2)}) collective-permute-start(f32[72,256]{1,0:T(8,128)S(1)} %get-tuple-element.26), channel_id=1, source_target_pairs={{1,2},{2,1},{3,31},{5,6},{6,5},{7,27},{9,10},{10,9},{11,23},{13,14... | collective-permute-start | bytes 221192 | tf_op jit(solution)/shard_map/ppermute | solution.py:797
  12.5 8.3 %collective-permute-start.2 = (f32[408,128]{1,0:T(8,128)S(1)}, f32[408,128]{1,0:T(8,128)S(1)}, u32[]{:S(2)}, u32[]{:S(2)}) collective-permute-start(f32[408,128]{1,0:T(8,128)S(1)} %get-tuple-element.36.refs_3_), channel_id=1, source_target_pairs={{0,28},{4,8},{8,4},{12,16},{16,12},{20,24},{24,20},{28,0},{1,29},{... | collective-permute-start | bytes 626696 | tf_op jit(solution)/shard_map/ppermute | solution.py:801
  13.8 6.9 %collective-permute-start.3 = (f32[408,128]{1,0:T(8,128)S(1)}, f32[408,128]{1,0:T(8,128)S(1)}, u32[]{:S(2)}, u32[]{:S(2)}) collective-permute-start(f32[408,128]{1,0:T(8,128)S(1)} %get-tuple-element.37.refs_4_), channel_id=1, source_target_pairs={{0,4},{4,0},{8,12},{12,8},{16,20},{20,16},{24,28},{28,24},{1,5},{5... | collective-permute-start | bytes 626696 | tf_op jit(solution)/shard_map/ppermute | solution.py:800
